TPU v7x, 512 devices: a whole 4x4x16 slice. The times are simulated.
512 devices in a mesh: view: 32 (over y, z_lo, core), row: 16 (over z_hi, x).
Axes of the slice: x: 4, y: 4, z: 16 (z_hi: 4, z_lo: 4; z = z_hi * 4 + z_lo), core: 2. Of those that a mesh axis runs over, the one named last changes fastest.
Arguments:
- queries: bfloat16 [32, 64, 64, 2048], P('view', 'row'), may hold values from -60 to 60
- target_keys: bfloat16 [32, 64, 64, 2048], P('view', 'row'), may hold values from -6 to 6
- target_values: bfloat16 [32, 64, 64, 2048], P('view', 'row'), may hold values from -6 to 6
- cond_keys: bfloat16 [512, 2048], P(('view', 'row')), may hold values from -21 to 21
- cond_values: bfloat16 [512, 2048], P(('view', 'row')), may hold values from -6 to 6
Outputs:
- attended: bfloat16 [32, 64, 64, 2048], P('view', 'row')
All inputs are finite; a program needn't handle non-finite values.
Results may differ from a plain program's by a relative error of at most 0.0089.
Values may be sent and summed in bfloat16 or wider, within the bound.
A program may use at most 64 MiB of HBM per device.

v0:
```python
import jax
import jax.numpy as jnp
from jax import lax
from jax.sharding import PartitionSpec as P

HD = 128
RADIUS = 8


BASE = 10000.0
NEG_FILL = -1e30


def side_by_side(arrays, axis, dim, along):
    ends, at = ([], 0)
    for a in arrays[:-1]:
        at += a.shape[along]
        ends.append(at)
    both = jnp.concatenate(arrays, axis=along)
    return tuple(jnp.split(lax.all_gather(both, axis, axis=dim, tiled=True), ends, axis=along))


def group_layout(head_dim):
    view_width = head_dim // 4
    row_width = 3 * head_dim // 8
    return (
        (0, view_width),
        (view_width, row_width),
        (view_width + row_width, head_dim - view_width - row_width),
    )


def rotary(features, coords):
    outputs = []
    for group_index, (offset, group_width) in enumerate(group_layout(features.shape[-1])):
        half_width = group_width // 2
        lower_part = features[..., offset : offset + half_width]
        upper_part = features[..., offset + half_width : offset + group_width]
        frequency = jnp.power(BASE, -jnp.arange(half_width, dtype=jnp.float32) / half_width)
        angles = coords[..., group_index][..., None, None] * frequency
        cosine = jnp.cos(angles)
        sine = jnp.sin(angles)
        outputs.append(lower_part * cosine - upper_part * sine)
        outputs.append(upper_part * cosine + lower_part * sine)
    return jnp.concatenate(outputs, axis=-1)


def attend(head_queries, head_keys, head_values, allowed, cond_head_keys, cond_head_values):
    scale = HD ** (-0.5)
    scores = jnp.dot(head_queries, head_keys.T, preferred_element_type=jnp.float32) * scale
    scores = jnp.where(allowed, scores, NEG_FILL)
    cond_scores = (
        jnp.dot(head_queries, cond_head_keys.T, preferred_element_type=jnp.float32) * scale
    )
    row_max = jnp.maximum(jnp.max(scores, axis=-1), jnp.max(cond_scores, axis=-1))
    weights = jnp.exp(scores - row_max[:, None])
    cond_weights = jnp.exp(cond_scores - row_max[:, None])
    denominator = jnp.sum(weights, axis=-1) + jnp.sum(cond_weights, axis=-1)
    summed = jnp.dot(weights.astype(jnp.bfloat16), head_values, preferred_element_type=jnp.float32)
    summed = summed + jnp.dot(
        cond_weights.astype(jnp.bfloat16), cond_head_values, preferred_element_type=jnp.float32
    )
    return summed / denominator[:, None]


def window_mask(query_count, key_count, cols, query_first, key_first, total_rows):
    query_ids = jnp.arange(query_count, dtype=jnp.int32)
    key_ids = jnp.arange(key_count, dtype=jnp.int32)
    query_row = query_first + query_ids // cols
    query_col = query_ids % cols
    key_row = key_first + key_ids // cols
    key_col = key_ids % cols
    allowed = (jnp.abs(query_row[:, None] - key_row[None, :]) <= RADIUS) & (
        jnp.abs(query_col[:, None] - key_col[None, :]) <= RADIUS
    )
    return allowed & ((key_row >= 0) & (key_row < total_rows))[None, :]


def largest_divisor(total, target):
    best = 1
    for candidate in range(1, total + 1):
        if total % candidate == 0 and candidate <= target:
            best = candidate
    return best


def local(queries, target_keys, target_values, cond_keys, cond_values):
    view_dev, rows_dev, cols, width = queries.shape
    heads = width // HD
    row_count = lax.axis_size("row")
    total_rows = rows_dev * row_count
    row_base = lax.axis_index("row") * rows_dev
    grid_shape = (view_dev, rows_dev, cols)
    view_coord = (
        lax.axis_index("view") * view_dev + jnp.arange(view_dev, dtype=jnp.int32) + 1
    ).astype(jnp.float32)
    row_coord = (row_base + jnp.arange(rows_dev, dtype=jnp.int32)).astype(jnp.float32)
    col_coord = jnp.arange(cols, dtype=jnp.int32).astype(jnp.float32)
    coords = jnp.stack(
        [
            jnp.broadcast_to(view_coord[:, None, None], grid_shape),
            jnp.broadcast_to(row_coord[None, :, None], grid_shape),
            jnp.broadcast_to(col_coord[None, None, :], grid_shape),
        ],
        axis=-1,
    )
    q_rot = rotary(
        queries.astype(jnp.float32).reshape(view_dev, rows_dev, cols, heads, HD), coords
    ).astype(jnp.bfloat16)
    k_rot = rotary(
        target_keys.astype(jnp.float32).reshape(view_dev, rows_dev, cols, heads, HD), coords
    ).astype(jnp.bfloat16)
    flat_queries = q_rot.reshape(view_dev, rows_dev, cols, width)
    flat_keys = k_rot.reshape(view_dev, rows_dev, cols, width)
    ctok_dev = cond_keys.shape[0]
    cond_base = (lax.axis_index("view") * row_count + lax.axis_index("row")) * ctok_dev
    cond_index = cond_base + jnp.arange(ctok_dev, dtype=jnp.int32)
    cond_coords = jnp.stack(
        [
            jnp.zeros((ctok_dev,), jnp.float32),
            (cond_index // cols).astype(jnp.float32),
            (cond_index % cols).astype(jnp.float32),
        ],
        axis=-1,
    )
    cond_rot = (
        rotary(cond_keys.astype(jnp.float32).reshape(ctok_dev, heads, HD), cond_coords)
        .astype(jnp.bfloat16)
        .reshape(ctok_dev, width)
    )
    group_keys, group_values = side_by_side((cond_rot, cond_values), "row", 0, 1)
    whole_keys, whole_values = side_by_side((group_keys, group_values), "view", 0, 1)
    ctok = whole_keys.shape[0]
    cond_key_heads = whole_keys.reshape(ctok, heads, HD)
    cond_value_heads = whole_values.reshape(ctok, heads, HD)
    own_heads = heads // row_count
    head_first = lax.axis_index("row") * own_heads
    moved_q, moved_k, moved_v = (
        lax.all_to_all(flat_queries, "row", split_axis=3, concat_axis=1, tiled=True),
        lax.all_to_all(flat_keys, "row", split_axis=3, concat_axis=1, tiled=True),
        lax.all_to_all(target_values, "row", split_axis=3, concat_axis=1, tiled=True),
    )
    cond_k = lax.dynamic_slice_in_dim(cond_key_heads, head_first, own_heads, 1).transpose(1, 0, 2)
    cond_v = lax.dynamic_slice_in_dim(cond_value_heads, head_first, own_heads, 1).transpose(1, 0, 2)
    padding = ((0, 0), (RADIUS, RADIUS), (0, 0), (0, 0))
    keys_pad = jnp.pad(moved_k, padding)
    values_pad = jnp.pad(moved_v, padding)
    block_rows = largest_divisor(total_rows, max(rows_dev, 512 // cols))
    band_rows = block_rows + 2 * RADIUS

    def one_block(block_id):
        first = block_id * block_rows
        block_q = (
            lax.dynamic_slice_in_dim(moved_q, first, block_rows, 1)
            .reshape(view_dev, block_rows * cols, own_heads, HD)
            .transpose(2, 0, 1, 3)
        )
        band_k = (
            lax.dynamic_slice_in_dim(keys_pad, first, band_rows, 1)
            .reshape(view_dev, band_rows * cols, own_heads, HD)
            .transpose(2, 0, 1, 3)
        )
        band_v = (
            lax.dynamic_slice_in_dim(values_pad, first, band_rows, 1)
            .reshape(view_dev, band_rows * cols, own_heads, HD)
            .transpose(2, 0, 1, 3)
        )
        allowed = window_mask(
            block_rows * cols, band_rows * cols, cols, first, first - RADIUS, total_rows
        )

        def one_head(operands):
            head_queries, head_keys, head_values, ck_head, cv_head = operands
            return jax.vmap(lambda a, b, c: attend(a, b, c, allowed, ck_head, cv_head))(
                head_queries, head_keys, head_values
            )

        out = lax.map(one_head, (block_q, band_k, band_v, cond_k, cond_v))
        return (
            out.transpose(1, 2, 0, 3)
            .reshape(view_dev, block_rows, cols, own_heads * HD)
            .astype(jnp.bfloat16)
        )

    blocks = lax.map(one_block, jnp.arange(total_rows // block_rows, dtype=jnp.int32))
    gathered_rows = blocks.transpose(1, 0, 2, 3, 4).reshape(
        view_dev, total_rows, cols, own_heads * HD
    )
    return lax.all_to_all(gathered_rows, "row", split_axis=1, concat_axis=3, tiled=True)


def solution(mesh):
    return jax.shard_map(
        local,
        mesh=mesh,
        in_specs=(
            P("view", "row", None, None),
            P("view", "row", None, None),
            P("view", "row", None, None),
            P(("view", "row"), None),
            P(("view", "row"), None),
        ),
        out_specs=P("view", "row", None, None),
        check_vma=False,
    )
```

profile of v0, /device:TPU:33, one launch (start us, length us, event | category | flops | bytes accessed | tf_op | source)
XLA Modules:
  0.0 428.1 jit_solution(3512994178728620318)
XLA Ops:
  6.6 4.5 %copy.43 = f32[1,4,64,2048]{2,1,3,0:T(4,128)} copy(bf16[1,4,64,2048]{3,2,1,0:T(8,128)(2,1)} %param.7) | data formatting | bytes 3145728 | tf_op jit(solution)/shard_map/reshape | solution.py:108
  11.1 2.8 copy.44
  14.0 2.2 fusion.50
  16.2 2.0 fusion.51
  19.0 2.4 fusion.44
  24.7 2.2 reshape.425
  26.9 16.6 %all-to-all-start.1 = ((bf16[16,2,16384]{2,1,0:T(2,128)(2,1)}), bf16[16,2,16384]{2,1,0:T(2,128)(2,1)S(1)}, u32[]{:S(2)}, u32[]{:S(2)}) async-start(bf16[16,2,16384]{2,1,0:T(2,128)(2,1)} %reshape.425), calls=%async_computation.1 | async-start | bytes 2097152 | tf_op jit(solution)/shard_map/all_to_all | solution.py:140
  44.1 88.7 %all-gather = bf16[16,1,4096]{2,1,0:T(2,128)(2,1)S(1)} all-gather(bf16[1,1,4096]{2,1,0:T(2,128)(2,1)S(1)} %maximum_bitcast_fusion), channel_id=1, replica_groups=mesh['view'=32,'row'=16] {'row'}, dimensions={0}, use_global_device_ids=true | all-gather | bytes 139264 | tf_op jit(solution)/shard_map/all_gather | solution.py:20
  133.6 2.2 reshape.423
  135.9 5.3 %all-to-all-start = ((bf16[16,2,16384]{2,1,0:T(2,128)(2,1)}), bf16[16,2,16384]{2,1,0:T(2,128)(2,1)}, u32[]{:S(2)}, u32[]{:S(2)}) async-start(bf16[16,2,16384]{2,1,0:T(2,128)(2,1)} %reshape.423), calls=%async_computation | async-start | bytes 2097152 | tf_op jit(solution)/shard_map/all_to_all | solution.py:139
  141.2 2.9 copy.36
  144.1 2.2 reshape.427
  146.4 43.9 %all-to-all-done = bf16[16,2,16384]{2,1,0:T(2,128)(2,1)} async-done(((bf16[16,2,16384]{2,1,0:T(2,128)(2,1)}), bf16[16,2,16384]{2,1,0:T(2,128)(2,1)}, u32[]{:S(2)}, u32[]{:S(2)}) %all-to-all-start) | async-done | bytes 1048608 | tf_op jit(solution)/shard_map/all_to_all | solution.py:139
  190.2 17.2 %all-to-all-start.2 = ((bf16[16,2,16384]{2,1,0:T(2,128)(2,1)}), bf16[16,2,16384]{2,1,0:T(2,128)(2,1)}, u32[]{:S(2)}, u32[]{:S(2)}) async-start(bf16[16,2,16384]{2,1,0:T(2,128)(2,1)} %reshape.427), calls=%async_computation.2 | async-start | bytes 2097152 | tf_op jit(solution)/shard_map/all_to_all | solution.py:141
  211.6 4.5 %reshape.424 = bf16[2048,1,4,64]{3,2,1,0:T(4,128)(2,1)S(1)} reshape(bf16[16,2,16384]{2,1,0:T(2,128)(2,1)} %all-to-all-done) | data formatting | bytes 2097152
  218.7 18.0 %all-to-all-done.2 = bf16[16,2,16384]{2,1,0:T(2,128)(2,1)} async-done(((bf16[16,2,16384]{2,1,0:T(2,128)(2,1)}), bf16[16,2,16384]{2,1,0:T(2,128)(2,1)}, u32[]{:S(2)}, u32[]{:S(2)}) %all-to-all-start.2) | async-done | bytes 1048608 | tf_op jit(solution)/shard_map/all_to_all | solution.py:141
  236.7 4.5 %reshape.428 = bf16[2048,1,4,64]{3,2,1,0:T(4,128)(2,1)S(1)} reshape(bf16[16,2,16384]{2,1,0:T(2,128)(2,1)} %all-to-all-done.2) | data formatting | bytes 2097152
  245.0 27.3 %all-gather.3.cloned.1.call-done = bf16[512,4096]{1,0:T(8,128)(2,1)} async-done(((bf16[16,4096]{1,0:T(8,128)(2,1)}), bf16[512,4096]{1,0:T(8,128)(2,1)}) %all-gather.3.cloned.1.call-update) | async-done | bytes 4194320 | tf_op jit(solution)/shard_map/all_gather | solution.py:20
  272.2 4.1 fusion.54
  276.3 3.9 copy.34
  282.9 2.5 copy.38
  286.4 65.2 %while.17 = (s32[]{:T(128)}, bf16[8,1,8,64,128]{4,3,2,1,0:T(8,128)(2,1)}, s32[8]{0:T(128)S(1)}, bf16[1,64,64,128]{3,2,1,0:T(8,128)(2,1)}, bf16[1,80,64,128]{3,2,...) while((s32[]{:T(128)}, ...), condition=%wide.region_5.6_spmd, body=%wide.region_0.5_spmd.sunk | while | flops 550480896 | bytes 16713464 | solution.py:185
  306.1 2.0 fusion.84
  351.7 68.3 %all_to_all.72 = bf16[1,64,64,128]{3,2,0,1:T(8,128)(2,1)S(1)} all-to-all(bf16[1,64,64,128]{3,2,0,1:T(8,128)(2,1)} %bitcast.117), channel_id=1, replica_groups=mesh['view'=32,'row'=16] {'row'}, dimensions={1} | all-to-all | bytes 2097152 | tf_op jit(solution)/shard_map/all_to_all | solution.py:189
  (169 shorter events, 77.9 us)
Async XLA Ops:
  6.5 4.5 %copy-start.4 = (bf16[1,4,64,2048]{3,2,1,0:T(8,128)(2,1)S(1)}, bf16[1,4,64,2048]{3,2,1,0:T(8,128)(2,1)}, u32[]{:S(2)}) copy-start(bf16[1,4,64,2048]{3,2,1,0:T(8,128)(2,1)} %param.8) | copy-start | bytes 3145732
  14.0 5.0 %copy-start = (f32[1,4,64,2048]{2,1,3,0:T(4,128)S(1)}, f32[1,4,64,2048]{2,1,3,0:T(4,128)}, u32[]{:S(2)}) copy-start(f32[1,4,64,2048]{2,1,3,0:T(4,128)} %copy.43) | copy-start | bytes 6291460
  18.2 3.2 copy-start.1
  23.3 1.3 copy-start.2
  24.7 18.9 %copy-start.5 = (bf16[1,2048]{1,0:T(2,128)(2,1)S(1)}, bf16[1,2048]{1,0:T(2,128)(2,1)}, u32[]{:S(2)}) copy-start(bf16[1,2048]{1,0:T(2,128)(2,1)} %param.10) | copy-start | bytes 12292
  24.7 19.4 %copy-start.6 = (bf16[1,2048]{1,0:T(2,128)(2,1)S(1)}, bf16[1,2048]{1,0:T(2,128)(2,1)}, u32[]{:S(2)}) copy-start(bf16[1,2048]{1,0:T(2,128)(2,1)} %param.11) | copy-start | bytes 12292
  26.9 106.7 %copy-start.3 = (bf16[1,4,64,16,128]{2,1,4,3,0:T(4,128)(2,1)S(1)}, bf16[1,4,64,16,128]{2,1,4,3,0:T(4,128)(2,1)}, u32[]{:S(2)}) copy-start(bf16[1,4,64,16,128]{2,1,4,3,0:T(4,128)(2,1)} %copy-done.2) | copy-start | bytes 3145732
  26.9 109.0 %all-to-all-start.1 = ((bf16[16,2,16384]{2,1,0:T(2,128)(2,1)}), bf16[16,2,16384]{2,1,0:T(2,128)(2,1)S(1)}, u32[]{:S(2)}, u32[]{:S(2)}) async-start(bf16[16,2,16384]{2,1,0:T(2,128)(2,1)} %reshape.425), calls=%async_computation.1 | async-start | bytes 2097152 | tf_op jit(solution)/shard_map/all_to_all | solution.py:140
  43.5 228.7 %all-gather.3.cloned.1.call-start = ((), (), s32[]{:S(2)}) async-start(), calls=%async_computation.4 | async-start | bytes 4325376 | tf_op jit(solution)/shard_map/all_gather | solution.py:20
  135.9 54.4 %all-to-all-start = ((bf16[16,2,16384]{2,1,0:T(2,128)(2,1)}), bf16[16,2,16384]{2,1,0:T(2,128)(2,1)}, u32[]{:S(2)}, u32[]{:S(2)}) async-start(bf16[16,2,16384]{2,1,0:T(2,128)(2,1)} %reshape.423), calls=%async_computation | async-start | bytes 2097152 | tf_op jit(solution)/shard_map/all_to_all | solution.py:139
  190.2 46.5 %all-to-all-start.2 = ((bf16[16,2,16384]{2,1,0:T(2,128)(2,1)}), bf16[16,2,16384]{2,1,0:T(2,128)(2,1)}, u32[]{:S(2)}, u32[]{:S(2)}) async-start(bf16[16,2,16384]{2,1,0:T(2,128)(2,1)} %reshape.427), calls=%async_computation.2 | async-start | bytes 2097152 | tf_op jit(solution)/shard_map/all_to_all | solution.py:141
Sparse Core Ops, SparseCore 0:
  133.8 138.4 all-gather.2
where the time goes:
time: 429 us; the launch traced here: 428 us
  blocking collectives  157 us (37%)
  waiting for transfers between devices  89.2 us (21%)
  local copies, waits for them, and re-layouts  80.5 us (19%)
  starting transfers between devices  39.2 us (9%)
  matrix products  26.3 us (6%)
  other arithmetic  16.1 us (4%)
  between operations  13.7 us (3%)
  loops' own time  6.1 us (1%)
    all_gather x1, blocking collectives, side_by_side(): lax.all_gather(both, axis, axis=dim, tiled=True)  88.7 us
    all_to_all x1, blocking collectives, local(): lax.all_to_all(gathered_rows, 'row', split_axis=1, concat_axis=3, tiled=T...  68.3 us
    all_to_all x1, waiting for transfers between devices, local(): lax.all_to_all(flat_queries, 'row', split_axis=3, concat_axis=1, tiled=True)  43.9 us
    all_gather x1, waiting for transfers between devices, side_by_side(): lax.all_gather(both, axis, axis=dim, tiled=True)  27.3 us
    unnamed x23, local copies, waits for them, and re-layouts  22.1 us
    all_to_all x1, waiting for transfers between devices, local(): lax.all_to_all(target_values, 'row', split_axis=3, concat_axis=1, tiled=T...  18 us
    all_to_all x1, starting transfers between devices, local(): lax.all_to_all(target_values, 'row', split_axis=3, concat_axis=1, tiled=T...  17.2 us
    all_to_all x1, starting transfers between devices, local(): lax.all_to_all(flat_keys, 'row', split_axis=3, concat_axis=1, tiled=True)  16.6 us
  transfers between devices with their start and end apart: 4, of which 3 were waited for; matrix products, arithmetic and copies ran while one was open for 7% of the time, Pallas kernels for 0%

commit v1 on v0

v1 whole, which is shorter than its diff:
```python
import functools
import math

import jax
import jax.numpy as jnp
import numpy as np
from jax import lax
from jax.experimental import pallas as pl
from jax.experimental.pallas import tpu as pltpu
from jax.sharding import PartitionSpec as P

HD = 128
RADIUS = 8
BASE = 10000.0
BIG = 1e30
COLS = 64
NX = 4
NZ = 4
NL = 4
NY = 4
RD = 4
HG = 4
LR = RD * NX
BR = LR + 2 * RADIUS
CT = 512
V, K, Q, O = range(4)
F32 = jnp.float32
BF16 = jnp.bfloat16


def trig_tables(views, rows, cols):
    widths = (HD // 4, 3 * HD // 8, 3 * HD // 8)
    counts = (views + 8, rows, cols)
    tables, offset = [], 0
    for width, count in zip(widths, counts):
        half = width // 2
        freq = np.power(np.float32(BASE), -np.arange(half, dtype=np.float32) / np.float32(half)).astype(np.float32)
        angle = (np.arange(count, dtype=np.float32)[:, None] * freq).astype(np.float64)
        table = np.zeros((2, count, HD), np.float32)
        for i, f in enumerate((np.cos, np.sin)):
            table[i, :, offset : offset + half] = f(angle)
            table[i, :, offset + half : offset + width] = f(angle)
        tables.append(table)
        offset += width
    return tables


def swap_matrix():
    swap, offset = np.zeros((HD, HD), np.float32), 0
    for width in (HD // 4, 3 * HD // 8, 3 * HD // 8):
        half = width // 2
        for i in range(offset, offset + half):
            swap[i + half, i] = -1.0
            swap[i, i + half] = 1.0
        offset += width
    return swap


def kernel(
    q_hbm, k_hbm, v_hbm, ck_ref, cv_ref, vt, rt, ct, swap, out_hbm,
    kin, qin, kst, qst, k_buf, v_buf, q_buf, o_buf, qaug, kaug, cs, cst, c1, ckv,
    lsem, xs, xr, zs, zr, c1s, c1r, ls, lr, ys, yr, ks, kr,
):
    row = lax.axis_index("row")
    view = lax.axis_index("view")
    x, zh = row % NX, row // NX
    core, zl, y = view % 2, (view // 2) % NL, view // (2 * NL)

    def row_dev(zz, xx):
        return {"view": view, "row": zz * NX + xx}

    def view_dev(yy, ll, cc):
        return {"view": (yy * NL + ll) * 2 + cc, "row": row}

    def remote(src, dst, s, r, dev):
        return pltpu.make_async_remote_copy(
            src_ref=src, dst_ref=dst, send_sem=s, recv_sem=r, device_id=dev, device_id_type=pl.DeviceIdType.MESH
        )

    load_k = pltpu.make_async_copy(k_hbm.at[0], kin, lsem.at[0])
    load_q = pltpu.make_async_copy(q_hbm.at[0], qin, lsem.at[1])
    load_k.start()
    load_q.start()

    barrier = pltpu.get_barrier_semaphore()

    def greet(dev):
        pl.semaphore_signal(barrier, inc=1, device_id=dev, device_id_type=pl.DeviceIdType.MESH)

    @pl.loop(1, NX * NZ)
    def _(d):
        greet({"view": view, "row": (row + d) % (NX * NZ)})

    for d in range(1, NL):
        greet(view_dev(y, (zl + d) % NL, core))
    for d in range(1, NY):
        greet(view_dev((y + d) % NY, zl, core))
    greet(view_dev(y, zl, 1 - core))

    for edge, first in ((0, 0), (NZ - 1, RADIUS + LR)):

        @pl.when(zh == edge)
        def _():
            @pl.loop(0, HG)
            def _(h):
                @pl.loop(0, RADIUS)
                def _(r):
                    k_buf[h, first + r] = jnp.zeros((COLS, HD), BF16)
                    v_buf[h, first + r] = jnp.zeros((COLS, HD), BF16)

    for i in range(2):
        base = ct[i] + vt[i, pl.ds(view + 1, 1), :]
        for r in range(RD):
            cs[i, pl.ds(r * COLS, COLS), :] = base + rt[i, pl.ds(row * RD + r, 1), :]

    for h in range(HG * NX):
        p, hh = h // HG, h % HG
        cst[pl.ds(p * 8 + hh, 1), :] = ck_ref[:, pl.ds(h * HD, HD)].astype(F32)
        cst[pl.ds(p * 8 + HG + hh, 1), :] = cv_ref[:, pl.ds(h * HD, HD)].astype(F32)
    token = view * (NX * NZ) + row
    ctok = [vt[i, pl.ds(0, 1), :] + rt[i, pl.ds(token // COLS, 1), :] + ct[i, pl.ds(token % COLS, 1), :] for i in range(2)]
    ckin = cst[...]
    crot = jnp.dot(ckin.astype(BF16), swap[...], preferred_element_type=F32)
    crot = (ckin * ctok[0] + crot * ctok[1]).astype(BF16).astype(F32)
    is_key = lax.broadcasted_iota(jnp.int32, (8 * NX, HD), 0) % 8 < HG
    cst[...] = jnp.where(is_key, crot, ckin)
    c1[pl.ds(pl.multiple_of(row * 8, 8), 8), :] = cst[pl.ds(pl.multiple_of(x * 8, 8), 8), :]

    pl.semaphore_wait(barrier, NX * NZ - 1 + NL - 1 + NY - 1 + 1)

    def own_rows(buf, h, xx):
        return buf.at[h, pl.ds(RADIUS + RD * xx, RD)]

    def x_src(kind, h, p):
        if kind == V:
            return v_hbm.at[0, :, :, pl.ds(pl.multiple_of((HG * p + h) * HD, HD), HD)]
        return (kst if kind == K else qst).at[p, h]

    def x_dst(kind, h, xx):
        if kind == Q:
            return q_buf.at[h, pl.ds(RD * xx, RD)]
        return own_rows(k_buf if kind == K else v_buf, h, xx)

    def x_copy(kind, h, d):
        p = (x + d) % NX
        return remote(x_src(kind, h, p), x_dst(kind, h, x), xs.at[kind, h, p], xr.at[kind, h, x], row_dev(zh, p))

    def x_own(kind, h):
        return pltpu.make_async_copy(x_src(kind, h, x), x_dst(kind, h, x), xs.at[kind, h, x])

    def x_send(kind, h):
        for d in (2, 1, 3):
            x_copy(kind, h, d).start()
        x_own(kind, h).start()

    def x_wait(kind, h):
        for d in (1, 2, 3):
            p = (x + d) % NX
            remote(x_src(kind, h, x), x_dst(kind, h, p), xs.at[kind, h, x], xr.at[kind, h, p], row_dev(zh, p)).wait_recv()
        x_own(kind, h).wait()

    def rope(src, dst, h):
        @pl.loop(0, NX)
        def _(p):
            feats = src[:, :, pl.ds(pl.multiple_of((HG * p + h) * HD, HD), HD)].reshape(RD * COLS, HD)
            turned = jnp.dot(feats, swap[...], preferred_element_type=F32)
            out = feats.astype(F32) * cs[0] + turned * cs[1]
            dst[p, h] = out.astype(BF16).reshape(RD, COLS, HD)

    def z_copy(kind, h, up):
        buf = k_buf if kind == K else v_buf
        src = buf.at[h, pl.ds(LR if up else RADIUS, RADIUS)]
        dst = buf.at[h, pl.ds(0 if up else RADIUS + LR, RADIUS)]
        return remote(src, dst, zs.at[up, kind, h], zr.at[up, kind, h], row_dev(zh + (1 if up else -1), x))

    def z_both(kind, h, act_up, act_down):
        pl.when(zh < NZ - 1)(lambda: act_up(z_copy(kind, h, 1)))
        pl.when(zh > 0)(lambda: act_down(z_copy(kind, h, 0)))

    def forward(kind, h):
        x_wait(kind, h)
        z_both(kind, h, lambda c: c.start(), lambda c: c.start())

    def c1_copy(d):
        peer = (row + d) % (NX * NZ)
        return remote(
            cst.at[pl.ds(pl.multiple_of((peer % NX) * 8, 8), 8), :],
            c1.at[pl.ds(pl.multiple_of(row * 8, 8), 8), :],
            c1s.at[peer], c1r.at[row], {"view": view, "row": peer},
        )

    def c1_wait(d):
        peer = (row + d) % (NX * NZ)
        remote(
            cst.at[pl.ds(0, 8), :],
            c1.at[pl.ds(pl.multiple_of(peer * 8, 8), 8), :],
            c1s.at[peer], c1r.at[peer], {"view": view, "row": peer},
        ).wait_recv()

    def slot(yy, ll, cc, blocks):
        return ckv.at[:, pl.ds(pl.multiple_of(((cc * NY + yy) * NL + ll) * 16, 16), blocks * 16), :]

    def l_copy(d):
        peer = (zl + d) % NL
        return remote(slot(y, zl, core, 1), slot(y, zl, core, 1), ls.at[peer], lr.at[zl], view_dev(y, peer, core))

    def l_wait(d):
        peer = (zl + d) % NL
        remote(slot(y, zl, core, 1), slot(y, peer, core, 1), ls.at[peer], lr.at[peer], view_dev(y, peer, core)).wait_recv()

    def y_copy(d):
        peer = (y + d) % NY
        return remote(slot(y, 0, core, NL), slot(y, 0, core, NL), ys.at[peer], yr.at[y], view_dev(peer, zl, core))

    def y_wait(d):
        peer = (y + d) % NY
        remote(slot(y, 0, core, NL), slot(peer, 0, core, NL), ys.at[peer], yr.at[peer], view_dev(peer, zl, core)).wait_recv()

    def core_copy(cc):
        return remote(slot(0, 0, cc, NL * NY), slot(0, 0, cc, NL * NY), ks.at[0], kr.at[0], view_dev(y, zl, 1 - core))

    x_send(V, 0)
    pl.loop(1, NX * NZ)(lambda d: c1_copy(d).start())
    load_k.wait()
    for h in range(HG):
        if h:
            x_send(V, h)
        rope(kin, kst, h)
        x_send(K, h)

    @pl.loop(0, LR)
    def _(r):
        lane = lax.broadcasted_iota(jnp.int32, (COLS, HD), 1)
        col = lax.broadcasted_iota(jnp.int32, (COLS, HD), 0)
        low = jnp.where(zh == 0, 80, -1)
        high = jnp.where(zh == NZ - 1, 81, -1)
        on = (lane == col) | (lane == r + COLS) | (lane == low) | (lane == high)
        qaug[r] = jnp.where(on, 1.0, 0.0).astype(BF16)

    @pl.loop(0, BR)
    def _(r):
        lane = lax.broadcasted_iota(jnp.int32, (COLS, HD), 1)
        col = lax.broadcasted_iota(jnp.int32, (COLS, HD), 0)
        low = jnp.where(r < RADIUS, 80, -1)
        high = jnp.where(r >= RADIUS + LR, 81, -1)
        far_col = (lane < COLS) & (jnp.abs(lane - col) > RADIUS)
        apart = r - (lane - COLS)
        far_row = (lane >= COLS) & (lane < COLS + LR) & ((apart < 0) | (apart > 2 * RADIUS))
        off = far_col | far_row | (lane == low) | (lane == high)
        kaug[r] = jnp.where(off, -BIG, 0.0).astype(BF16)

    forward(V, 0)
    forward(K, 0)
    pl.loop(1, NX * NZ)(c1_wait)
    for i in range(8):
        rows16 = c1[pl.ds(i, NX * NZ, stride=8), :]
        ckv[i, pl.ds(pl.multiple_of(((core * NY + y) * NL + zl) * 16, 16), 16), :] = rows16.astype(BF16)
    for d in range(1, NL):
        l_copy(d).start()
    load_q.wait()
    for h in range(HG):
        rope(qin, qst, h)
        x_send(Q, h)
    forward(V, 1)
    forward(K, 1)
    for d in range(1, NL):
        l_wait(d)
    for d in range(1, NY):
        y_copy(d).start()
    forward(V, 2)
    forward(K, 2)
    for d in range(1, NY):
        y_wait(d)
    core_copy(core).start()
    forward(V, 3)
    forward(K, 3)
    core_copy(1 - core).wait_recv()

    def o_copy(h, b):
        return remote(
            o_buf.at[h, pl.ds(RD * b, RD)],
            out_hbm.at[0, :, :, pl.ds(pl.multiple_of((HG * x + h) * HD, HD), HD)],
            xs.at[O, h, b], xr.at[O, h, x], row_dev(zh, b),
        )

    def o_own(h):
        return pltpu.make_async_copy(
            o_buf.at[h, pl.ds(RD * x, RD)],
            out_hbm.at[0, :, :, pl.ds(pl.multiple_of((HG * x + h) * HD, HD), HD)],
            xs.at[O, h, x],
        )

    def o_wait(h, p):
        remote(
            o_buf.at[h, pl.ds(RD * p, RD)],
            out_hbm.at[0, :, :, pl.ds(pl.multiple_of((HG * p + h) * HD, HD), HD)],
            xs.at[O, h, p], xr.at[O, h, p], row_dev(zh, p),
        ).wait_recv()

    scale = math.log2(math.e) / math.sqrt(HD)
    nt = (((1,), (1,)), ((), ()))

    def block(h, b):
        n, band = RD * COLS, (RD + 2 * RADIUS) * COLS
        qb = q_buf[h, pl.ds(RD * b, RD)].reshape(n, HD)
        qa = qaug[pl.ds(RD * b, RD)].reshape(n, HD)
        kb = k_buf[h, pl.ds(RD * b, RD + 2 * RADIUS)].reshape(band, HD)
        ka = kaug[pl.ds(RD * b, RD + 2 * RADIUS)].reshape(band, HD)
        s1 = lax.dot_general(
            jnp.concatenate([qb, qa], axis=1), jnp.concatenate([kb, ka], axis=1), nt, preferred_element_type=F32
        )
        s2 = lax.dot_general(qb, ckv[h], nt, preferred_element_type=F32)
        m = jnp.maximum(jnp.max(s1, axis=1, keepdims=True), jnp.max(s2, axis=1, keepdims=True))
        p1 = jnp.exp2((s1 - m) * scale).astype(BF16)
        p2 = jnp.exp2((s2 - m) * scale).astype(BF16)
        vb = v_buf[h, pl.ds(RD * b, RD + 2 * RADIUS)].reshape(band, HD)
        acc = jnp.dot(p1, jnp.concatenate([vb, jnp.ones((band, HD), BF16)], axis=1), preferred_element_type=F32)
        acc += jnp.dot(
            p2, jnp.concatenate([ckv[HG + h], jnp.ones((CT, HD), BF16)], axis=1), preferred_element_type=F32
        )
        o_buf[h, pl.ds(RD * b, RD)] = (acc[:, :HD] / acc[:, HD:]).astype(BF16).reshape(RD, COLS, HD)

    @pl.loop(0, HG)
    def _(h):
        x_wait(Q, h)
        for kind in (V, K):
            pl.when(zh > 0)(lambda: z_copy(kind, h, 1).wait_recv())
            pl.when(zh < NZ - 1)(lambda: z_copy(kind, h, 0).wait_recv())

        @pl.loop(1, NX)
        def _(d):
            b = (x + d) % NX
            block(h, b)
            o_copy(h, b).start()

        block(h, x)
        o_own(h).start()

    @pl.loop(0, HG)
    def _(h):
        for d in range(1, NX):
            p = (x + d) % NX
            o_wait(h, p)
            o_copy(h, p).wait_send()
            for kind in (V, K, Q):
                x_copy(kind, h, d).wait_send()
        o_own(h).wait()
        for kind in (V, K):
            z_both(kind, h, lambda c: c.wait_send(), lambda c: c.wait_send())

    pl.loop(1, NX * NZ)(lambda d: c1_copy(d).wait_send())
    for d in range(1, NL):
        l_copy(d).wait_send()
    for d in range(1, NY):
        y_copy(d).wait_send()
    core_copy(core).wait_send()


def local(queries, target_keys, target_values, cond_keys, cond_values):
    rows = queries.shape[1] * NX * NZ
    views = 2 * NL * NY
    vt, rt, ct = trig_tables(views, rows, COLS)
    vmem, hbm = pl.BlockSpec(memory_space=pltpu.VMEM), pl.BlockSpec(memory_space=pl.ANY)
    heads = HG * NX
    dma = pltpu.SemaphoreType.DMA
    return pl.pallas_call(
        kernel,
        out_shape=jax.ShapeDtypeStruct(queries.shape, BF16),
        in_specs=[hbm] * 3 + [vmem] * 6,
        out_specs=hbm,
        scratch_shapes=[
            pltpu.VMEM((RD, COLS, heads * HD), BF16),
            pltpu.VMEM((RD, COLS, heads * HD), BF16),
            pltpu.VMEM((NX, HG, RD, COLS, HD), BF16),
            pltpu.VMEM((NX, HG, RD, COLS, HD), BF16),
            pltpu.VMEM((HG, BR, COLS, HD), BF16),
            pltpu.VMEM((HG, BR, COLS, HD), BF16),
            pltpu.VMEM((HG, LR, COLS, HD), BF16),
            pltpu.VMEM((HG, LR, COLS, HD), BF16),
            pltpu.VMEM((LR, COLS, HD), BF16),
            pltpu.VMEM((BR, COLS, HD), BF16),
            pltpu.VMEM((2, RD * COLS, HD), F32),
            pltpu.VMEM((8 * NX, HD), F32),
            pltpu.VMEM((8 * NX * NZ, HD), F32),
            pltpu.VMEM((2 * HG, CT, HD), BF16),
            dma((2,)),
            dma((4, HG, NX)),
            dma((4, HG, NX)),
            dma((2, 2, HG)),
            dma((2, 2, HG)),
            dma((NX * NZ,)),
            dma((NX * NZ,)),
            dma((NL,)),
            dma((NL,)),
            dma((NY,)),
            dma((NY,)),
            dma((1,)),
            dma((1,)),
        ],
        compiler_params=pltpu.CompilerParams(
            collective_id=0, has_side_effects=True, vmem_limit_bytes=48 * 1024 * 1024
        ),
        cost_estimate=pl.CostEstimate(flops=8_000_000_000, bytes_accessed=5_000_000, transcendentals=8_000_000),
    )(
        queries, target_keys, target_values, cond_keys, cond_values,
        jnp.asarray(vt), jnp.asarray(rt), jnp.asarray(ct), jnp.asarray(swap_matrix(), BF16),
    )


def solution(mesh):
    return jax.shard_map(
        local,
        mesh=mesh,
        in_specs=(
            P("view", "row", None, None),
            P("view", "row", None, None),
            P("view", "row", None, None),
            P(("view", "row"), None),
            P(("view", "row"), None),
        ),
        out_specs=P("view", "row", None, None),
        check_vma=False,
    )
```

time: 429 us -> 138 us (0.32)
  the two profiles are of different devices: /device:TPU:33 before, /device:TPU:262 now
where the time goes in v1:
time: 138 us
  Pallas kernels  129 us (93%)
  local copies, waits for them, and re-layouts  9.25 us (7%)
    pallas_call x1, Pallas kernels, local(): pl.pallas_call(kernel, out_shape=jax.ShapeDtypeStruct(queries.shape, BF16...  129 us
    unnamed x19, local copies, waits for them, and re-layouts  9.25 us

profile of v1, /device:TPU:262, one launch (start us, length us, event | category | flops | bytes accessed | tf_op | source)
XLA Modules:
  0.0 137.9 jit_solution(13024378444753149884)
XLA Ops:
  0.0 0.0 copy-start
  0.0 1.2 copy-done
  1.2 0.0 copy-start.1
  1.2 1.2 copy-done.1
  2.5 0.0 copy-start.2
  2.5 1.2 copy-done.2
  3.7 0.0 copy-start.3
  3.7 0.7 copy-done.3
  4.4 0.0 copy-start.4
  4.4 0.7 copy-done.4
  5.1 0.0 copy-start.5
  5.1 0.8 copy-done.5
  5.9 0.0 copy-start.6
  5.9 0.8 copy-done.6
  6.8 0.0 copy-start.7
  6.8 0.8 copy-done.7
  7.5 0.0 copy-start.8
  7.5 0.8 copy-done.8
  8.3 128.6 %shard_map.91 = bf16[1,4,64,2048]{3,2,1,0:T(8,128)(2,1)S(1)} custom-call(bf16[1,4,64,2048]{3,2,1,0:T(8,128)(2,1)S(1)} %copy-done, bf16[1,4,64,2048]{3,2,1,0:T(8,128)(2,1)S(1)} %copy-done.1, bf16[1,4,64,2048]{3,2,1,0:T(8,128)(2,1)S(1)} %copy-done.2, bf16[1,2048]{1,0:T(2,128)(2,1)S(1)} %copy-done.3, bf16[1,2048]{1,0:T(2,128)(2,1)S(1)} %copy-done.4, ...), custom_call_target="tpu_custom_call" | custom-call | flops 8000000000 | bytes 5000000 | tf_op jit(solution)/shard_map/pallas_call | solution.py:366
  136.9 1.0 copy.11
Async XLA Ops:
  0.0 1.2 copy-start
  1.2 1.2 copy-start.1
  2.5 1.2 copy-start.2
  3.7 0.7 copy-start.3
  4.4 0.7 copy-start.4
  5.1 0.8 copy-start.5
  5.9 0.8 copy-start.6
  6.8 0.8 copy-start.7
  7.5 0.8 copy-start.8

commit v2 on v1

v2 whole, which is shorter than its diff:
```python
import functools
import math

import jax
import jax.numpy as jnp
import numpy as np
from jax import lax
from jax.experimental import pallas as pl
from jax.experimental.pallas import tpu as pltpu
from jax.sharding import PartitionSpec as P

HD = 128
RADIUS = 8
BASE = 10000.0
BIG = 1e30
COLS = 64
NX = 4
NZ = 4
NL = 4
NY = 4
RD = 4
HG = 4
LR = RD * NX
BR = LR + 2 * RADIUS
CT = 512
ROWS = LR * NZ
VIEW_ROWS = 40
VIEW_TAB, ROW_TAB, COL_TAB, SWAP_TAB = 0, 2 * VIEW_ROWS, 2 * (VIEW_ROWS + ROWS), 2 * (VIEW_ROWS + ROWS + COLS)
V, K, Q, O = range(4)
F32 = jnp.float32
BF16 = jnp.bfloat16


def trig_tables(rows, cols):
    widths = (HD // 4, 3 * HD // 8, 3 * HD // 8)
    counts = (VIEW_ROWS, rows, cols)
    tables, offset = [], 0
    for width, count in zip(widths, counts):
        half = width // 2
        freq = np.power(np.float32(BASE), -np.arange(half, dtype=np.float32) / np.float32(half)).astype(np.float32)
        angle = (np.arange(count, dtype=np.float32)[:, None] * freq).astype(np.float64)
        table = np.zeros((2, count, HD), np.float32)
        for i, f in enumerate((np.cos, np.sin)):
            table[i, :, offset : offset + half] = f(angle)
            table[i, :, offset + half : offset + width] = f(angle)
        tables.append(table)
        offset += width
    return tables


def swap_matrix():
    swap, offset = np.zeros((HD, HD), np.float32), 0
    for width in (HD // 4, 3 * HD // 8, 3 * HD // 8):
        half = width // 2
        for i in range(offset, offset + half):
            swap[i + half, i] = -1.0
            swap[i, i + half] = 1.0
        offset += width
    return swap


def kernel(
    q_hbm, k_hbm, v_hbm, ck_hbm, cv_hbm, tab_hbm, out_hbm,
    tab, swap, ck_ref, cv_ref, kin, qin, kst, qst, k_buf, v_buf, q_buf, o_buf, qaug, kaug, cs, cst, c1, ckv,
    lsem, xs, xr, zs, zr, c1s, c1r, ls, lr, ys, yr, ks, kr,
):
    row = lax.axis_index("row")
    view = lax.axis_index("view")
    x, zh = row % NX, row // NX
    core, zl, y = view % 2, (view // 2) % NL, view // (2 * NL)

    def row_dev(zz, xx):
        return {"view": view, "row": zz * NX + xx}

    def view_dev(yy, ll, cc):
        return {"view": (yy * NL + ll) * 2 + cc, "row": row}

    def remote(src, dst, s, r, dev):
        return pltpu.make_async_remote_copy(
            src_ref=src, dst_ref=dst, send_sem=s, recv_sem=r, device_id=dev, device_id_type=pl.DeviceIdType.MESH
        )

    barrier = pltpu.get_barrier_semaphore()

    def greet(dev):
        pl.semaphore_signal(barrier, inc=1, device_id=dev, device_id_type=pl.DeviceIdType.MESH)

    @pl.loop(1, NX * NZ)
    def _(d):
        greet({"view": view, "row": (row + d) % (NX * NZ)})

    for d in range(1, NL):
        greet(view_dev(y, (zl + d) % NL, core))
    for d in range(1, NY):
        greet(view_dev((y + d) % NY, zl, core))
    greet(view_dev(y, zl, 1 - core))

    loads = [
        pltpu.make_async_copy(src, dst, lsem.at[i])
        for i, (src, dst) in enumerate(
            ((tab_hbm, tab), (ck_hbm, ck_ref), (cv_hbm, cv_ref), (k_hbm.at[0], kin), (q_hbm.at[0], qin))
        )
    ]
    for load in loads:
        load.start()

    pl.semaphore_wait(barrier, NX * NZ - 1 + NL - 1 + NY - 1 + 1)

    def own_rows(buf, h, xx):
        return buf.at[h, pl.ds(RADIUS + RD * xx, RD)]

    def x_src(kind, h, p):
        if kind == V:
            return v_hbm.at[0, :, :, pl.ds(pl.multiple_of((HG * p + h) * HD, HD), HD)]
        return (kst if kind == K else qst).at[p, h]

    def x_dst(kind, h, xx):
        if kind == Q:
            return q_buf.at[h, pl.ds(RD * xx, RD)]
        return own_rows(k_buf if kind == K else v_buf, h, xx)

    def x_copy(kind, h, d):
        p = (x + d) % NX
        return remote(x_src(kind, h, p), x_dst(kind, h, x), xs.at[kind, h, p], xr.at[kind, h, x], row_dev(zh, p))

    def x_own(kind, h):
        return pltpu.make_async_copy(x_src(kind, h, x), x_dst(kind, h, x), xs.at[kind, h, x])

    def x_send(kind, h):
        for d in (2, 1, 3):
            x_copy(kind, h, d).start()
        x_own(kind, h).start()

    def x_from(kind, h, p):
        @pl.when(p != x)
        def _():
            remote(x_src(kind, h, x), x_dst(kind, h, p), xs.at[kind, h, x], xr.at[kind, h, p], row_dev(zh, p)).wait_recv()

        @pl.when(p == x)
        def _():
            x_own(kind, h).wait()

    def rope(src, dst, h):
        @pl.loop(0, NX)
        def _(p):
            feats = src[:, :, pl.ds(pl.multiple_of((HG * p + h) * HD, HD), HD)].reshape(RD * COLS, HD)
            turned = jnp.dot(feats, swap[...], preferred_element_type=F32)
            out = feats.astype(F32) * cs[0] + turned * cs[1]
            dst[p, h] = out.astype(BF16).reshape(RD, COLS, HD)

    def z_copy(kind, h, up, far):
        buf = k_buf if kind == K else v_buf
        if up:
            src, dst = RADIUS + LR - RD * (1 + far), RD * (1 - far)
        else:
            src, dst = RADIUS + RD * far, RADIUS + LR + RD * far
        i = 2 * up + far
        return remote(
            buf.at[h, pl.ds(src, RD)], buf.at[h, pl.ds(dst, RD)],
            zs.at[i, kind, h], zr.at[i, kind, h], row_dev(zh + (1 if up else -1), x),
        )

    has_up, has_down = zh < NZ - 1, zh > 0

    def forward(kind, h):
        for far in (0, 1):
            x_from(kind, h, NX - 1 - far)
            pl.when(has_up)(lambda: z_copy(kind, h, 1, far).start())
            x_from(kind, h, far)
            pl.when(has_down)(lambda: z_copy(kind, h, 0, far).start())

    def c1_copy(d):
        peer = (row + d) % (NX * NZ)
        return remote(
            cst.at[pl.ds(pl.multiple_of((peer % NX) * 8, 8), 8), :],
            c1.at[pl.ds(pl.multiple_of(row * 8, 8), 8), :],
            c1s.at[peer], c1r.at[row], {"view": view, "row": peer},
        )

    def c1_wait(d):
        peer = (row + d) % (NX * NZ)
        remote(
            cst.at[pl.ds(0, 8), :],
            c1.at[pl.ds(pl.multiple_of(peer * 8, 8), 8), :],
            c1s.at[peer], c1r.at[peer], {"view": view, "row": peer},
        ).wait_recv()

    def slot(yy, ll, cc, blocks):
        return ckv.at[:, pl.ds(pl.multiple_of(((cc * NY + yy) * NL + ll) * 16, 16), blocks * 16), :]

    def l_copy(d):
        peer = (zl + d) % NL
        return remote(slot(y, zl, core, 1), slot(y, zl, core, 1), ls.at[peer], lr.at[zl], view_dev(y, peer, core))

    def l_wait(d):
        peer = (zl + d) % NL
        remote(slot(y, zl, core, 1), slot(y, peer, core, 1), ls.at[peer], lr.at[peer], view_dev(y, peer, core)).wait_recv()

    def y_copy(d):
        peer = (y + d) % NY
        return remote(slot(y, 0, core, NL), slot(y, 0, core, NL), ys.at[peer], yr.at[y], view_dev(peer, zl, core))

    def y_wait(d):
        peer = (y + d) % NY
        remote(slot(y, 0, core, NL), slot(peer, 0, core, NL), ys.at[peer], yr.at[peer], view_dev(peer, zl, core)).wait_recv()

    def core_copy(cc):
        return remote(slot(0, 0, cc, NL * NY), slot(0, 0, cc, NL * NY), ks.at[0], kr.at[0], view_dev(y, zl, 1 - core))

    x_send(V, 0)
    for load in loads[:3]:
        load.wait()
    swap[...] = tab[pl.ds(SWAP_TAB, HD), :].astype(BF16)

    for i in range(2):
        base = tab[pl.ds(COL_TAB + i * COLS, COLS), :] + tab[pl.ds(VIEW_TAB + i * VIEW_ROWS + view + 1, 1), :]
        for r in range(RD):
            cs[i, pl.ds(r * COLS, COLS), :] = base + tab[pl.ds(ROW_TAB + i * ROWS + row * RD + r, 1), :]

    for h in range(HG * NX):
        p, hh = h // HG, h % HG
        cst[pl.ds(p * 8 + hh, 1), :] = ck_ref[:, pl.ds(h * HD, HD)].astype(F32)
        cst[pl.ds(p * 8 + HG + hh, 1), :] = cv_ref[:, pl.ds(h * HD, HD)].astype(F32)
    token = view * (NX * NZ) + row
    ctok = [
        tab[pl.ds(VIEW_TAB + i * VIEW_ROWS, 1), :]
        + tab[pl.ds(ROW_TAB + i * ROWS + token // COLS, 1), :]
        + tab[pl.ds(COL_TAB + i * COLS + token % COLS, 1), :]
        for i in range(2)
    ]
    ckin = cst[...]
    crot = jnp.dot(ckin.astype(BF16), swap[...], preferred_element_type=F32)
    crot = (ckin * ctok[0] + crot * ctok[1]).astype(BF16).astype(F32)
    is_key = lax.broadcasted_iota(jnp.int32, (8 * NX, HD), 0) % 8 < HG
    cst[...] = jnp.where(is_key, crot, ckin)
    c1[pl.ds(pl.multiple_of(row * 8, 8), 8), :] = cst[pl.ds(pl.multiple_of(x * 8, 8), 8), :]

    pl.loop(1, NX * NZ)(lambda d: c1_copy(d).start())
    for edge, first in ((0, 0), (NZ - 1, RADIUS + LR)):

        @pl.when(zh == edge)
        def _():
            @pl.loop(0, HG)
            def _(h):
                @pl.loop(0, RADIUS)
                def _(r):
                    k_buf[h, first + r] = jnp.zeros((COLS, HD), BF16)
                    v_buf[h, first + r] = jnp.zeros((COLS, HD), BF16)

    loads[3].wait()
    rope(kin, kst, 0)
    x_send(K, 0)
    x_send(V, 1)
    forward(V, 0)
    rope(kin, kst, 1)
    x_send(K, 1)
    forward(K, 0)
    pl.loop(1, NX * NZ)(c1_wait)
    for i in range(8):
        rows16 = c1[pl.ds(i, NX * NZ, stride=8), :]
        ckv[i, pl.ds(pl.multiple_of(((core * NY + y) * NL + zl) * 16, 16), 16), :] = rows16.astype(BF16)
    for d in range(1, NL):
        l_copy(d).start()
    x_send(V, 2)
    rope(kin, kst, 2)
    x_send(K, 2)
    forward(V, 1)
    forward(K, 1)
    x_send(V, 3)
    rope(kin, kst, 3)
    x_send(K, 3)
    forward(V, 2)
    loads[4].wait()
    for h in range(HG):
        rope(qin, qst, h)
        x_send(Q, h)
    forward(K, 2)
    forward(V, 3)
    forward(K, 3)

    @pl.loop(0, LR)
    def _(r):
        lane = lax.broadcasted_iota(jnp.int32, (COLS, HD), 1)
        col = lax.broadcasted_iota(jnp.int32, (COLS, HD), 0)
        low = jnp.where(zh == 0, 80, -1)
        high = jnp.where(zh == NZ - 1, 81, -1)
        on = (lane == col) | (lane == r + COLS) | (lane == low) | (lane == high)
        qaug[r] = jnp.where(on, 1.0, 0.0).astype(BF16)

    @pl.loop(0, BR)
    def _(r):
        lane = lax.broadcasted_iota(jnp.int32, (COLS, HD), 1)
        col = lax.broadcasted_iota(jnp.int32, (COLS, HD), 0)
        low = jnp.where(r < RADIUS, 80, -1)
        high = jnp.where(r >= RADIUS + LR, 81, -1)
        far_col = (lane < COLS) & (jnp.abs(lane - col) > RADIUS)
        apart = r - (lane - COLS)
        far_row = (lane >= COLS) & (lane < COLS + LR) & ((apart < 0) | (apart > 2 * RADIUS))
        off = far_col | far_row | (lane == low) | (lane == high)
        kaug[r] = jnp.where(off, -BIG, 0.0).astype(BF16)

    for d in range(1, NL):
        l_wait(d)
    for d in range(1, NY):
        y_copy(d).start()
    for d in range(1, NY):
        y_wait(d)
    core_copy(core).start()
    core_copy(1 - core).wait_recv()

    def o_copy(h, b):
        return remote(
            o_buf.at[h, pl.ds(RD * b, RD)],
            out_hbm.at[0, :, :, pl.ds(pl.multiple_of((HG * x + h) * HD, HD), HD)],
            xs.at[O, h, b], xr.at[O, h, x], row_dev(zh, b),
        )

    def o_own(h):
        return pltpu.make_async_copy(
            o_buf.at[h, pl.ds(RD * x, RD)],
            out_hbm.at[0, :, :, pl.ds(pl.multiple_of((HG * x + h) * HD, HD), HD)],
            xs.at[O, h, x],
        )

    def o_wait(h, p):
        remote(
            o_buf.at[h, pl.ds(RD * p, RD)],
            out_hbm.at[0, :, :, pl.ds(pl.multiple_of((HG * p + h) * HD, HD), HD)],
            xs.at[O, h, p], xr.at[O, h, p], row_dev(zh, p),
        ).wait_recv()

    scale = math.log2(math.e) / math.sqrt(HD)
    nt = (((1,), (1,)), ((), ()))

    def block(h, b):
        n, band = RD * COLS, (RD + 2 * RADIUS) * COLS
        qb = q_buf[h, pl.ds(RD * b, RD)].reshape(n, HD)
        qa = qaug[pl.ds(RD * b, RD)].reshape(n, HD)
        kb = k_buf[h, pl.ds(RD * b, RD + 2 * RADIUS)].reshape(band, HD)
        ka = kaug[pl.ds(RD * b, RD + 2 * RADIUS)].reshape(band, HD)
        s1 = lax.dot_general(
            jnp.concatenate([qb, qa], axis=1), jnp.concatenate([kb, ka], axis=1), nt, preferred_element_type=F32
        )
        s2 = lax.dot_general(qb, ckv[h], nt, preferred_element_type=F32)
        m = jnp.maximum(jnp.max(s1, axis=1, keepdims=True), jnp.max(s2, axis=1, keepdims=True))
        p1 = jnp.exp2((s1 - m) * scale).astype(BF16)
        p2 = jnp.exp2((s2 - m) * scale).astype(BF16)
        vb = v_buf[h, pl.ds(RD * b, RD + 2 * RADIUS)].reshape(band, HD)
        acc = jnp.dot(p1, jnp.concatenate([vb, jnp.ones((band, HD), BF16)], axis=1), preferred_element_type=F32)
        acc += jnp.dot(
            p2, jnp.concatenate([ckv[HG + h], jnp.ones((CT, HD), BF16)], axis=1), preferred_element_type=F32
        )
        o_buf[h, pl.ds(RD * b, RD)] = (acc[:, :HD] / acc[:, HD:]).astype(BF16).reshape(RD, COLS, HD)

    @pl.loop(0, HG)
    def _(h):
        for p in range(NX):
            x_from(Q, h, p)
        for b in (1, 2, 0, 3):
            up, far = b < NX // 2, b in (0, NX - 1)
            for kind in (V, K):
                pl.when(has_down if up else has_up)(lambda: z_copy(kind, h, up, far).wait_recv())
            block(h, b)
            pl.when(x != b)(lambda: o_copy(h, b).start())
            pl.when(x == b)(lambda: o_own(h).start())

    @pl.loop(0, HG)
    def _(h):
        for d in range(1, NX):
            p = (x + d) % NX
            o_wait(h, p)
            o_copy(h, p).wait_send()
            for kind in (V, K, Q):
                x_copy(kind, h, d).wait_send()
        o_own(h).wait()
        for kind in (V, K):
            for far in (0, 1):
                pl.when(has_up)(lambda: z_copy(kind, h, 1, far).wait_send())
                pl.when(has_down)(lambda: z_copy(kind, h, 0, far).wait_send())

    pl.loop(1, NX * NZ)(lambda d: c1_copy(d).wait_send())
    for d in range(1, NL):
        l_copy(d).wait_send()
    for d in range(1, NY):
        y_copy(d).wait_send()
    core_copy(core).wait_send()


def local(queries, target_keys, target_values, cond_keys, cond_values):
    rows = queries.shape[1] * NX * NZ
    tables = [t.reshape(-1, HD) for t in trig_tables(rows, COLS)] + [swap_matrix()]
    tables = np.concatenate(tables)
    hbm = pl.BlockSpec(memory_space=pltpu.HBM)
    heads = HG * NX
    dma = pltpu.SemaphoreType.DMA
    return pl.pallas_call(
        kernel,
        out_shape=jax.ShapeDtypeStruct(queries.shape, BF16),
        in_specs=[hbm] * 6,
        out_specs=hbm,
        scratch_shapes=[
            pltpu.VMEM(tables.shape, F32),
            pltpu.VMEM((HD, HD), BF16),
            pltpu.VMEM((1, heads * HD), BF16),
            pltpu.VMEM((1, heads * HD), BF16),
            pltpu.VMEM((RD, COLS, heads * HD), BF16),
            pltpu.VMEM((RD, COLS, heads * HD), BF16),
            pltpu.VMEM((NX, HG, RD, COLS, HD), BF16),
            pltpu.VMEM((NX, HG, RD, COLS, HD), BF16),
            pltpu.VMEM((HG, BR, COLS, HD), BF16),
            pltpu.VMEM((HG, BR, COLS, HD), BF16),
            pltpu.VMEM((HG, LR, COLS, HD), BF16),
            pltpu.VMEM((HG, LR, COLS, HD), BF16),
            pltpu.VMEM((LR, COLS, HD), BF16),
            pltpu.VMEM((BR, COLS, HD), BF16),
            pltpu.VMEM((2, RD * COLS, HD), F32),
            pltpu.VMEM((8 * NX, HD), F32),
            pltpu.VMEM((8 * NX * NZ, HD), F32),
            pltpu.VMEM((2 * HG, CT, HD), BF16),
            dma((5,)),
            dma((4, HG, NX)),
            dma((4, HG, NX)),
            dma((4, 2, HG)),
            dma((4, 2, HG)),
            dma((NX * NZ,)),
            dma((NX * NZ,)),
            dma((NL,)),
            dma((NL,)),
            dma((NY,)),
            dma((NY,)),
            dma((1,)),
            dma((1,)),
        ],
        compiler_params=pltpu.CompilerParams(
            collective_id=0, has_side_effects=True, vmem_limit_bytes=60 * 1024 * 1024
        ),
        cost_estimate=pl.CostEstimate(flops=8_000_000_000, bytes_accessed=5_000_000, transcendentals=8_000_000),
    )(
        queries, target_keys, target_values, cond_keys, cond_values, jnp.asarray(tables)
    )


def solution(mesh):
    return jax.shard_map(
        local,
        mesh=mesh,
        in_specs=(
            P("view", "row", None, None),
            P("view", "row", None, None),
            P("view", "row", None, None),
            P(("view", "row"), None),
            P(("view", "row"), None),
        ),
        out_specs=P("view", "row", None, None),
        check_vma=False,
    )
```

time: 138 us -> 127 us (0.920)
  the two profiles are of different devices: /device:TPU:262 before, /device:TPU:64 now
where the time goes in v2:
time: 127 us
  Pallas kernels  124 us (98%)
  local copies, waits for them, and re-layouts  2.3 us (2%)
    pallas_call x1, Pallas kernels, local(): pl.pallas_call(kernel, out_shape=jax.ShapeDtypeStruct(queries.shape, BF16...  124 us

profile of v2, /device:TPU:64, one launch (start us, length us, event | category | flops | bytes accessed | tf_op | source)
XLA Modules:
  0.0 126.7 jit_solution(7807369054671117590)
XLA Ops:
  0.0 124.4 %shard_map.64 = bf16[1,4,64,2048]{3,2,1,0:T(8,128)(2,1)} custom-call(bf16[1,4,64,2048]{3,2,1,0:T(8,128)(2,1)} %q_hbm.1, bf16[1,4,64,2048]{3,2,1,0:T(8,128)(2,1)} %k_hbm.1, bf16[1,4,64,2048]{3,2,1,0:T(8,128)(2,1)} %v_hbm.1, bf16[1,2048]{1,0:T(2,128)(2,1)} %ck_hbm.1, bf16[1,2048]{1,0:T(2,128)(2,1)} %cv_hbm.1, f32[464,128]{1,0:T(8,128)} %constant.2.clone.tab_hbm), custom_call_target="tpu_custom_call" | custom-call | flops 8000000000 | bytes 5000000 | tf_op jit(solution)/shard_map/pallas_call | solution.py:396
  124.4 2.3 %copy.8 = bf16[1,4,64,2048]{3,2,1,0:T(8,128)(2,1)} copy(bf16[1,4,64,2048]{3,2,1,0:T(8,128)(2,1)} %shard_map.64) | data formatting | bytes 2097152

commit v3 on v2

--- a/solution.py
+++ b/solution.py
@@ -104,7 +104,6 @@
     for load in loads:
         load.start()
 
-    pl.semaphore_wait(barrier, NX * NZ - 1 + NL - 1 + NY - 1 + 1)
 
     def own_rows(buf, h, xx):
         return buf.at[h, pl.ds(RADIUS + RD * xx, RD)]
@@ -207,7 +206,6 @@
     def core_copy(cc):
         return remote(slot(0, 0, cc, NL * NY), slot(0, 0, cc, NL * NY), ks.at[0], kr.at[0], view_dev(y, zl, 1 - core))
 
-    x_send(V, 0)
     for load in loads[:3]:
         load.wait()
     swap[...] = tab[pl.ds(SWAP_TAB, HD), :].astype(BF16)
@@ -235,7 +233,6 @@
     cst[...] = jnp.where(is_key, crot, ckin)
     c1[pl.ds(pl.multiple_of(row * 8, 8), 8), :] = cst[pl.ds(pl.multiple_of(x * 8, 8), 8), :]
 
-    pl.loop(1, NX * NZ)(lambda d: c1_copy(d).start())
     for edge, first in ((0, 0), (NZ - 1, RADIUS + LR)):
 
         @pl.when(zh == edge)
@@ -249,12 +246,16 @@
 
     loads[3].wait()
     rope(kin, kst, 0)
+    rope(kin, kst, 1)
+
+    pl.semaphore_wait(barrier, NX * NZ - 1 + NL - 1 + NY - 1 + 1)
+    x_send(V, 0)
+    pl.loop(1, NX * NZ)(lambda d: c1_copy(d).start())
+    forward(V, 0)
     x_send(K, 0)
+    forward(K, 0)
     x_send(V, 1)
-    forward(V, 0)
-    rope(kin, kst, 1)
     x_send(K, 1)
-    forward(K, 0)
     pl.loop(1, NX * NZ)(c1_wait)
     for i in range(8):
         rows16 = c1[pl.ds(i, NX * NZ, stride=8), :]

time: 127 us -> 126 us (level)
  the two profiles are of different devices: /device:TPU:64 before, /device:TPU:94 now
where the time goes in v3:
time: 126 us
  Pallas kernels  124 us (98%)
  local copies, waits for them, and re-layouts  2.3 us (2%)
    pallas_call x1, Pallas kernels, local(): pl.pallas_call(kernel, out_shape=jax.ShapeDtypeStruct(queries.shape, BF16...  124 us

profile of v3, /device:TPU:94, one launch (start us, length us, event | category | flops | bytes accessed | tf_op | source)
XLA Modules:
  0.0 126.0 jit_solution(4362133213972367905)
XLA Ops:
  0.0 123.7 %shard_map.64 = bf16[1,4,64,2048]{3,2,1,0:T(8,128)(2,1)} custom-call(bf16[1,4,64,2048]{3,2,1,0:T(8,128)(2,1)} %q_hbm.1, bf16[1,4,64,2048]{3,2,1,0:T(8,128)(2,1)} %k_hbm.1, bf16[1,4,64,2048]{3,2,1,0:T(8,128)(2,1)} %v_hbm.1, bf16[1,2048]{1,0:T(2,128)(2,1)} %ck_hbm.1, bf16[1,2048]{1,0:T(2,128)(2,1)} %cv_hbm.1, f32[464,128]{1,0:T(8,128)} %constant.2.clone.tab_hbm), custom_call_target="tpu_custom_call" | custom-call | flops 8000000000 | bytes 5000000 | tf_op jit(solution)/shard_map/pallas_call | solution.py:397
  123.7 2.3 %copy.8 = bf16[1,4,64,2048]{3,2,1,0:T(8,128)(2,1)} copy(bf16[1,4,64,2048]{3,2,1,0:T(8,128)(2,1)} %shard_map.64) | data formatting | bytes 2097152
